TPU v7x, 768 devices: a whole 4x8x12 slice. The times are simulated.
768 devices in a mesh: node: 12 (over x, z_hi), local: 64 (over y, z_lo, core).
Axes of the slice: x: 4, y: 8, z: 12 (z_hi: 3, z_lo: 4; z = z_hi * 4 + z_lo), core: 2. Of those that a mesh axis runs over, the one named last changes fastest.
Arguments:
- tokens: bfloat16 [196608, 8192], P(('node', 'local')), may hold values from -6 to 6
- cotangent: bfloat16 [196608, 128], P(('node', 'local')), may hold values from -0.013671875 to 0.013671875
- weight_codes: bfloat16 [8192, 128], P('local'), may hold values from -127 to 127, as said below
- weight_scales: bfloat16 [4096], P('local'), may hold values from 4.9829483e-05 to 0.00049972534
- rounding_table: int32 [8192, 128], replicated, may hold values from 0 to 1023
- stream_offsets: int32 [768], P(('node', 'local')), may hold values from 0 to 1023
Outputs:
- projected: bfloat16 [196608, 128], P(('node', 'local'))
- weight_grad: float32 [8192, 128], P('local')
Inputs may be any that keep to these rules, and one draw needn't show every extreme that they name: `weight_codes`: whole numbers.
All inputs are finite; a program needn't handle non-finite values.
Results may differ from a plain program's by a relative error of at most 0.012.
Values may be sent and summed in bfloat16 or wider, within the bound.
A program may use at most 64 MiB of HBM per device.

v0:
```python
import jax
import jax.numpy as jnp
from jax import lax
from jax.sharding import PartitionSpec as P

QB = 256


EPS = 1e-06
HEADROOM = 1.0078125
GRAD_TOP = 7.0
NODE_TOP = 127.0


def quantize(blocks, shift, top):
    largest = jnp.max(jnp.abs(blocks), axis=1)
    scale = ((largest + EPS) * HEADROOM / top).astype(jnp.bfloat16)
    codes = (blocks / scale.astype(jnp.float32)[:, None] + (shift - 0.5)).astype(jnp.bfloat16)
    return (codes, scale)


def dequantize(codes, scale):
    return codes.astype(jnp.float32) * scale.astype(jnp.float32)[..., None]


def on_device(tokens, cotangent, weight_codes, weight_scales, rounding_table, stream_offsets):
    width = weight_codes.shape[1]
    group = QB // width
    owners = lax.axis_size("local")
    own_blocks = weight_codes.shape[0] // group
    packed = weight_codes.reshape(own_blocks, QB)
    codes = lax.all_gather(packed, "local", axis=0, tiled=True)
    scales = lax.all_gather(weight_scales, "local", axis=0, tiled=True)
    count = codes.shape[0]
    dense = dequantize(codes, scales).astype(jnp.bfloat16).reshape(count * group, width)
    folded = jnp.dot(tokens, dense, preferred_element_type=jnp.float32)
    projected = folded.astype(jnp.bfloat16)
    partial_value = lax.dot_general(
        tokens, cotangent, (((0,), (0,)), ((), ())), preferred_element_type=jnp.float32
    )
    all_blocks = partial_value.reshape(own_blocks * owners, QB)
    offset = stream_offsets[0]
    shift = (jnp.remainder(rounding_table + offset, 1024).astype(jnp.float32) + 0.5) / 1024.0
    codes, scales = quantize(all_blocks, shift.reshape(own_blocks * owners, QB), GRAD_TOP)
    sent_codes = codes.reshape(owners, own_blocks, QB)
    sent_scales = scales.reshape(owners, own_blocks)
    got_codes, got_scales = (
        lax.all_to_all(sent_codes, "local", split_axis=0, concat_axis=0, tiled=True),
        lax.all_to_all(sent_scales, "local", split_axis=0, concat_axis=0, tiled=True),
    )
    node_total = jnp.sum(dequantize(got_codes, got_scales), axis=0)
    node_codes, node_scales = quantize(node_total, 0.5, NODE_TOP)
    summed = lax.psum(dequantize(node_codes, node_scales), "node")
    return (projected, summed.reshape(own_blocks * group, width))


def solution(mesh):
    in_specs = (
        P(("node", "local"), None),
        P(("node", "local"), None),
        P("local", None),
        P("local"),
        P(),
        P(("node", "local")),
    )
    out_specs = (P(("node", "local"), None), P("local", None))
    return jax.shard_map(
        on_device, mesh=mesh, in_specs=in_specs, out_specs=out_specs, check_vma=False
    )
```

profile of v0, /device:TPU:8, one launch (start us, length us, event | category | flops | bytes accessed | tf_op | source)
XLA Modules:
  0.0 416.3 jit_solution(4038725885001863662)
XLA Ops:
  8.0 0.0 copy-start
  8.0 0.8 copy-done
  8.8 4.9 %abs_reduce_fusion = (f32[8192]{0:T(1024)S(1)}, f32[8192,128]{0,1:T(8,128)}) fusion(bf16[256,8192]{1,0:T(8,128)(2,1)} %param.6, bf16[256,128]{1,0:T(8,128)(2,1)S(1)} %copy-done), kind=kOutput, calls=%fused_computation.10 | convolution fusion | flops 538959872 | bytes 8486912 | tf_op jit(solution)/shard_map/dot_general | solution.py:38
  13.7 2.1 reduce_max.26
  15.8 0.6 reduce_max.27
  16.5 0.7 convert_element_type.105
  17.2 13.5 %all-to-all-start.1 = ((bf16[64,1,64]{2,1,0:T(2,128)(2,1)}), bf16[64,1,64]{2,1,0:T(2,128)(2,1)S(1)}, u32[]{:S(2)}, u32[]{:S(2)}) async-start(bf16[64,1,64]{2,1,0:T(2,128)(2,1)} %convert_element_type.105), calls=%async_computation.1 | async-start | bytes 65536 | tf_op jit(solution)/shard_map/all_to_all | solution.py:49
  30.7 0.1 reshape.85
  30.8 5.6 %copy.13 = f32[8192,128]{1,0:T(8,128)} copy(f32[8192,128]{0,1:T(8,128)} %get-tuple-element.11) | data formatting | bytes 8388608 | tf_op jit(solution)/shard_map/dot_general | solution.py:38
  36.3 5.2 %reshape.83 = f32[64,64,256]{2,1,0:T(8,128)} reshape(f32[8192,128]{1,0:T(8,128)} %copy.13) | data formatting | bytes 8388608 | tf_op jit(solution)/shard_map/reshape | solution.py:41
  42.2 6.3 %fusion.4 = f32[8192,128]{1,0:T(8,128)} fusion(s32[8192,128]{1,0:T(8,128)} %param.10, s32[]{:T(128)} %bitcast.9), kind=kLoop, calls=%fused_computation.7 | loop fusion | flops 16777216 | bytes 8388612 | tf_op jit(solution)/shard_map/sub | solution.py:18
  48.5 5.2 %sub.7 = f32[64,64,256]{2,1,0:T(8,128)} reshape(f32[8192,128]{1,0:T(8,128)} %fusion.4) | data formatting | bytes 8388608 | tf_op jit(solution)/shard_map/sub | solution.py:18
  53.7 4.8 %add_convert_fusion = bf16[64,64,256]{2,1,0:T(8,128)(2,1)} fusion(f32[64,64,256]{2,1,0:T(8,128)} %sub.7, f32[64,64,256]{2,1,0:T(8,128)} %reshape.83, f32[64,64]{1,0:T(8,128)S(1)} %reshape.85), kind=kLoop, calls=%fused_computation.9 | loop fusion | flops 3145728 | bytes 10502144 | tf_op jit(solution)/shard_map/convert_element_type | solution.py:18
  58.5 0.0 copy-start.1
  58.5 0.0 copy-start.2
  58.5 0.0 all-to-all-done.1
  58.5 11.0 %all-to-all-start = ((bf16[64,64,256]{2,1,0:T(8,128)(2,1)}), bf16[64,64,256]{2,1,0:T(8,128)(2,1)}, u32[]{:S(2)}, u32[]{:S(2)}) async-start(bf16[64,64,256]{2,1,0:T(8,128)(2,1)} %add_convert_fusion), calls=%async_computation | async-start | bytes 4194304 | tf_op jit(solution)/shard_map/all_to_all | solution.py:48
  69.5 0.0 all-gather.2.cloned.1.call-start
  69.6 0.0 copy-done.1
  69.6 0.6 reshape.81
  70.2 0.0 all-gather.2.cloned.1.call-update
  70.3 0.0 all-reduce.3.cloned.1.call-start
  70.3 1.3 dynamic-slice
  72.3 0.0 copy-done.2
  72.3 0.2 dynamic-update-slice
  72.5 151.6 %all-reduce = bf16[4096]{0:T(1024)(128)(2,1)S(1)} all-reduce(bf16[4096]{0:T(1024)(128)(2,1)S(1)} %dynamic-update-slice), channel_id=1, replica_groups=mesh['node'=12,'local'=64] {'local'}, use_global_device_ids=true, to_apply=%add | all-reduce | flops 4096 | bytes 16384
  224.2 0.0 all-gather.2.cloned.1.call-done
  224.2 2.9 multiply_convert_fusion
  227.2 2.7 reshape.82
  229.9 0.0 all-to-all-done
  229.9 1.9 multiply_reduce_fusion
  231.8 0.1 abs_reduce_fusion.1
  231.9 0.1 convert_multiply_fusion
  232.0 0.6 reshape.84
  232.6 0.0 all-reduce.3.cloned.1.call-update
  232.7 3.7 fusion.5
  236.4 0.7 copy.15
  237.1 170.2 %all-reduce.3.cloned.1.call-done = f32[128,128]{1,0:T(8,128)} async-done(((f32[128,128]{1,0:T(8,128)}), f32[128,128]{1,0:T(8,128)}) %all-reduce.3.cloned.1.call-update) | async-done | bytes 65552 | tf_op jit(solution)/shard_map/psum | solution.py:53
  407.4 1.5 copy.19
  (5 shorter events, 0.1 us)
Async XLA Ops:
  8.0 0.8 copy-start
  17.2 41.4 %all-to-all-start.1 = ((bf16[64,1,64]{2,1,0:T(2,128)(2,1)}), bf16[64,1,64]{2,1,0:T(2,128)(2,1)S(1)}, u32[]{:S(2)}, u32[]{:S(2)}) async-start(bf16[64,1,64]{2,1,0:T(2,128)(2,1)} %convert_element_type.105), calls=%async_computation.1 | async-start | bytes 65536 | tf_op jit(solution)/shard_map/all_to_all | solution.py:49
  58.5 11.1 %copy-start.1 = (bf16[128,128]{1,0:T(8,128)(2,1)S(1)}, bf16[128,128]{1,0:T(8,128)(2,1)}, u32[]{:S(2)}) copy-start(bf16[128,128]{1,0:T(8,128)(2,1)} %param.8) | copy-start | bytes 98308
  58.5 13.8 %copy-start.2 = (bf16[64]{0:T(256)(128)(2,1)S(1)}, bf16[64]{0:T(256)(128)(2,1)}, u32[]{:S(2)}) copy-start(bf16[64]{0:T(256)(128)(2,1)} %param.9) | copy-start | bytes 388
  58.5 171.3 %all-to-all-start = ((bf16[64,64,256]{2,1,0:T(8,128)(2,1)}), bf16[64,64,256]{2,1,0:T(8,128)(2,1)}, u32[]{:S(2)}, u32[]{:S(2)}) async-start(bf16[64,64,256]{2,1,0:T(8,128)(2,1)} %add_convert_fusion), calls=%async_computation | async-start | bytes 4194304 | tf_op jit(solution)/shard_map/all_to_all | solution.py:48
  69.5 154.7 %all-gather.2.cloned.1.call-start = ((), (), s32[]{:S(2)}) async-start(), calls=%async_computation.2 | async-start | bytes 2129920 | tf_op jit(solution)/shard_map/all_gather | solution.py:32
  70.3 337.1 %all-reduce.3.cloned.1.call-start = ((), (), s32[]{:S(2)}) async-start(), calls=%async_computation.3 | async-start | bytes 131072 | tf_op jit(solution)/shard_map/psum | solution.py:53
Sparse Core Ops, SparseCore 0:
  73.4 136.1 all-gather.1
Sparse Core Ops, SparseCore 1:
  232.8 174.5 all-reduce.2
where the time goes:
time: 417 us; the launch traced here: 416 us
  waiting for transfers between devices  170 us (41%)
  blocking collectives  152 us (36%)
  local copies, waits for them, and re-layouts  27.3 us (7%)
  starting transfers between devices  24.6 us (6%)
  other arithmetic  16.9 us (4%)
  between operations  16.9 us (4%)
  matrix products  8.61 us (2%)
    psum x1, waiting for transfers between devices, on_device(): summed = lax.psum(dequantize(node_codes, node_scales), 'node')  170 us
    unnamed x1, blocking collectives  152 us
    all_to_all x1, starting transfers between devices, on_device(): lax.all_to_all(sent_scales, 'local', split_axis=0, concat_axis=0, tiled=T...  13.5 us
    all_to_all x1, starting transfers between devices, on_device(): lax.all_to_all(sent_codes, 'local', split_axis=0, concat_axis=0, tiled=True)  11 us
  transfers between devices with their start and end apart: 4, of which 1 were waited for; matrix products, arithmetic and copies ran while one was open for 9% of the time, Pallas kernels for 0%

commit v1 on v0

v1 whole, which is shorter than its diff:
```python
import jax
import jax.numpy as jnp
from jax import lax
from jax.experimental import pallas as pl
from jax.experimental.pallas import tpu as pltpu
from jax.sharding import PartitionSpec as P

MESH = pl.DeviceIdType.MESH
EPS = 1e-06
HEADROOM = 1.0078125
GRAD_TOP = 7.0
NODE_TOP = 127.0

NX, NZH, NY, NZ = 4, 3, 8, 4
HALF_Y = NY // 2
ROWS = 128
HD = 128
HB = ROWS // 2
CHUNK = NZ * 2 * ROWS
TOK = 256


def block_scale(even, odd, top):
    largest = jnp.max(jnp.maximum(jnp.abs(even), jnp.abs(odd)), axis=1, keepdims=True)
    return ((largest + EPS) * HEADROOM / top).astype(jnp.bfloat16).astype(jnp.float32)


def kernel(
    tok_hbm, cot_hbm, wc_hbm, ws_ref, table_hbm, off_ref,
    proj_ref, grad_ref,
    tok, cot, wc, table, part, own, sib_out, sib_in, r_out, r_in, l_out, l_in,
    z_out, z_in, h_buf, x_buf, w_buf,
    tok_sem, table_sem, small_sem, sib_ss, sib_rs, r_ss, r_rs, l_ss, l_rs,
    z_ss, z_rs, h_ss, h_rs, x_ss, x_rs, gz_ss, gz_rs, gr_ss, gr_rs, gl_ss, gl_rs, gs_ss, gs_rs,
):
    node = lax.axis_index("node")
    local = lax.axis_index("local")
    x, zh = node // NZH, node % NZH
    y, z, core = local // (NZ * 2), (local // 2) % NZ, local % 2
    other = 1 - core

    def at(y_, z_, c_):
        return (node, (y_ * NZ + z_) * 2 + c_)

    sibling = at(y, z, other)
    right = at((y + 1) % NY, z, core)
    left = at((y + NY - 1) % NY, z, core)
    z_peers = [at(y, (z + j) % NZ, core) for j in range(1, NZ)]
    h_peers = [(x * NZH + (zh + j) % NZH, local) for j in range(1, NZH)]
    x_peers = [(((x + j) % NX) * NZH + zh, local) for j in range(1, NX)]
    everyone = [sibling, right, left] + z_peers + h_peers + x_peers

    barrier = pltpu.get_barrier_semaphore()
    for peer in everyone:
        pl.semaphore_signal(barrier, inc=1, device_id=peer, device_id_type=MESH)

    order = [(y + HALF_Y) % NY]
    for far in range(HALF_Y - 1, 0, -1):
        order += [(y + far) % NY, (y + NY - far) % NY]
    order += [y]

    def tok_copy(k):
        cols = pl.ds(pl.multiple_of(order[k] * CHUNK, CHUNK), CHUNK)
        return pltpu.make_async_copy(tok_hbm.at[:, cols], tok.at[:, cols], tok_sem.at[k])

    def table_copy(k):
        rows = pl.ds(pl.multiple_of(order[k] * CHUNK, CHUNK), CHUNK)
        return pltpu.make_async_copy(table_hbm.at[rows], table.at[rows], table_sem.at[k])

    cot_copy = pltpu.make_async_copy(cot_hbm, cot, small_sem.at[0])
    wc_copy = pltpu.make_async_copy(wc_hbm, wc, small_sem.at[1])
    cot_copy.start()
    wc_copy.start()
    for k in range(NY):
        tok_copy(k).start()
        table_copy(k).start()

    def remote(src, dst, ss, rs, dev):
        return pltpu.make_async_remote_copy(
            src_ref=src, dst_ref=dst, send_sem=ss, recv_sem=rs, device_id=dev, device_id_type=MESH
        )

    wc_copy.wait()
    row = lax.broadcasted_iota(jnp.int32, (ROWS, HB), 0)
    col = lax.broadcasted_iota(jnp.int32, (ROWS, HB), 1)
    spread = jnp.broadcast_to(ws_ref[...].astype(jnp.float32), (ROWS, HB))
    w_scale = jnp.sum(jnp.where(row // 2 == col, spread, 0.0), axis=1, keepdims=True)
    w_buf[y, z, core] = (wc[...].astype(jnp.float32) * w_scale).astype(jnp.bfloat16)

    pl.semaphore_wait(barrier, len(everyone))

    mine = w_buf.at[y, z, core]
    gz = [remote(mine, mine, gz_ss.at[j], gz_rs.at[j], z_peers[j]) for j in range(NZ - 1)]
    for copy in gz:
        copy.start()

    offset = off_ref[0]
    cot_copy.wait()

    def quantized(block, core_of, base):
        start = pl.multiple_of((block * 2 + core_of) * ROWS, ROWS)
        even = part[pl.ds(start, HB, stride=2), :]
        odd = part[pl.ds(start + 1, HB, stride=2), :]
        scale = block_scale(even, odd, GRAD_TOP)
        inverse = 1.0 / scale
        out = []
        for parity, value in ((0, even), (1, odd)):
            draws = table[pl.ds(base + start + parity, HB, stride=2), :]
            draws = ((draws + offset) & 1023).astype(jnp.float32)
            shift = draws * (1.0 / 1024.0) + (0.5 / 1024.0 - 0.5)
            codes = (value * inverse + shift).astype(jnp.bfloat16)
            out.append(codes.astype(jnp.float32) * scale)
        return out

    def sib_copy(k):
        return remote(sib_out.at[k], sib_in.at[k], sib_ss.at[k], sib_rs.at[k], sibling)

    def compute(k):
        tok_copy(k).wait()
        table_copy(k).wait()
        base = pl.multiple_of(order[k] * CHUNK, CHUNK)
        part[...] = lax.dot_general(
            tok[:, pl.ds(base, CHUNK)], cot[...], (((0,), (0,)), ((), ())),
            preferred_element_type=jnp.float32,
        )
        for block in range(NZ):
            even, odd = quantized(block, other, base)
            sib_out[k, block, :HB] = even.astype(jnp.bfloat16)
            sib_out[k, block, HB:] = odd.astype(jnp.bfloat16)
        sib_copy(k).start()
        for block in range(NZ):
            even, odd = quantized(block, core, base)
            own[k, block, :HB] = even
            own[k, block, HB:] = odd

    def chip_sum(k):
        sib_copy(k).wait_recv()
        return own[k] + sib_in[k].astype(jnp.float32)

    HALF_Z = NZ // 2

    def r_copy(s):
        if s == 0:
            return remote(r_out.at[0, :HALF_Z], r_in.at[0, :HALF_Z], r_ss.at[0], r_rs.at[0], right)
        return remote(r_out.at[s], r_in.at[s], r_ss.at[s], r_rs.at[s], right)

    def l_copy(s):
        if s == 0:
            return remote(l_out.at[0, HALF_Z:], l_in.at[0, HALF_Z:], l_ss.at[0], l_rs.at[0], left)
        return remote(l_out.at[s], l_in.at[s], l_ss.at[s], l_rs.at[s], left)

    def pass_on(k):
        if k == 0:
            total = chip_sum(0).astype(jnp.bfloat16)
            r_out[0, :HALF_Z] = total[:HALF_Z]
            l_out[0, HALF_Z:] = total[HALF_Z:]
            r_copy(0).start()
            l_copy(0).start()
            return
        s = (k + 1) // 2
        total = chip_sum(k)
        copy, out, came = (r_copy, r_out, r_in) if k % 2 == 1 else (l_copy, l_out, l_in)
        copy(s - 1).wait_recv()
        if s == 1:
            low, high = (HALF_Z, NZ) if k % 2 == 1 else (0, HALF_Z)
            joined = (0, HALF_Z) if k % 2 == 1 else (HALF_Z, NZ)
            a, b = joined
            out[s, a:b] = (total[a:b] + came[0, a:b].astype(jnp.float32)).astype(jnp.bfloat16)
            out[s, low:high] = total[low:high].astype(jnp.bfloat16)
        else:
            out[s] = (total + came[s - 1].astype(jnp.float32)).astype(jnp.bfloat16)
        copy(s).start()

    for k in range(NY):
        compute(k)
        if k >= 1:
            pass_on(k - 1)

    def g_copy(way, s):
        if way == 0:
            b, ss, rs, dev = (y + NY - s) % NY, gr_ss, gr_rs, right
        else:
            b, ss, rs, dev = (y + s) % NY, gl_ss, gl_rs, left
        if s == HALF_Y - 1:
            src = w_buf.at[b, :HALF_Z, core] if way == 0 else w_buf.at[b, HALF_Z:, core]
        else:
            src = w_buf.at[b, :, core]
        return remote(src, src, ss.at[s], rs.at[s], dev)

    def g_came(way, s):
        if way == 0:
            b, ss, rs = (y + NY - s - 1) % NY, gr_ss, gr_rs
        else:
            b, ss, rs = (y + s + 1) % NY, gl_ss, gl_rs
        if s == HALF_Y - 1:
            dst = w_buf.at[b, :HALF_Z, core] if way == 0 else w_buf.at[b, HALF_Z:, core]
        else:
            dst = w_buf.at[b, :, core]
        return remote(dst, dst, ss.at[s], rs.at[s], sibling)

    def gs_copy(r):
        src = w_buf.at[(y + r) % NY, :, core]
        return remote(src, src, gs_ss.at[r], gs_rs.at[r], sibling)

    def gs_came(r):
        dst = w_buf.at[(y + r) % NY, :, other]
        return remote(dst, dst, gs_ss.at[r], gs_rs.at[r], sibling)

    for j in range(NZ - 1):
        src = w_buf.at[y, (z + NZ - 1 - j) % NZ, core]
        remote(src, src, gz_ss.at[j], gz_rs.at[j], sibling).wait_recv()
    g_copy(0, 0).start()
    g_copy(1, 0).start()
    gs_copy(0).start()

    total = chip_sum(NY - 1)
    r_copy(HALF_Y - 1).wait_recv()
    total += r_in[HALF_Y - 1].astype(jnp.float32)
    l_copy(HALF_Y - 1).wait_recv()
    total += l_in[HALF_Y - 1].astype(jnp.float32)
    own[NY - 1] = total
    z_out[...] = total.astype(jnp.bfloat16)

    def z_copy(j):
        return remote(
            z_out.at[(z + j + 1) % NZ], z_in.at[j], z_ss.at[j], z_rs.at[j], z_peers[j]
        )

    for j in range(NZ - 1):
        z_copy(j).start()

    def g_step(s):
        g_came(0, s).wait_recv()
        g_came(1, s).wait_recv()
        if s < HALF_Y - 1:
            g_copy(0, s + 1).start()
            g_copy(1, s + 1).start()
            gs_copy(NY - s - 1).start()
            gs_copy(s + 1).start()
        else:
            gs_copy(HALF_Y).start()

    g_step(0)

    node_total = own[NY - 1, z]
    for j in range(NZ - 1):
        z_copy(j).wait_recv()
        node_total += z_in[j].astype(jnp.float32)
    even, odd = node_total[:HB], node_total[HB:]
    scale = block_scale(even, odd, NODE_TOP)
    inverse = 1.0 / scale
    for at_row, value in ((0, even), (HB, odd)):
        codes = (value * inverse).astype(jnp.bfloat16)
        h_buf[zh, at_row:at_row + HB] = (codes.astype(jnp.float32) * scale).astype(jnp.bfloat16)

    def h_copy(j):
        return remote(h_buf.at[zh], h_buf.at[zh], h_ss.at[j], h_rs.at[j], h_peers[j])

    def h_came(j):
        dst = h_buf.at[(zh + NZH - 1 - j) % NZH]
        return remote(dst, dst, h_ss.at[j], h_rs.at[j], sibling)

    for j in range(NZH - 1):
        h_copy(j).start()

    g_step(1)

    for j in range(NZH - 1):
        h_came(j).wait_recv()
    summed = h_buf[0].astype(jnp.float32)
    for i in range(1, NZH):
        summed += h_buf[i].astype(jnp.float32)
    x_buf[x] = summed.astype(jnp.bfloat16)

    def x_copy(j):
        return remote(x_buf.at[x], x_buf.at[x], x_ss.at[j], x_rs.at[j], x_peers[j])

    def x_came(j):
        dst = x_buf.at[(x + NX - 1 - j) % NX]
        return remote(dst, dst, x_ss.at[j], x_rs.at[j], sibling)

    for j in range(NX - 1):
        x_copy(j).start()

    g_step(2)

    def term(r):
        gs_came(r).wait_recv()
        b = (y + r) % NY
        dense = w_buf[b].reshape(CHUNK, HD)
        cols = pl.ds(pl.multiple_of(b * CHUNK, CHUNK), CHUNK)
        return jnp.dot(tok[:, cols], dense, preferred_element_type=jnp.float32)

    projected = term(0)
    for s in range(1, HALF_Y - 1):
        projected += term(s)
        projected += term(NY - s)

    for j in range(NX - 1):
        x_came(j).wait_recv()
    summed = x_buf[0].astype(jnp.float32)
    for i in range(1, NX):
        summed += x_buf[i].astype(jnp.float32)
    grad_ref[pl.ds(0, HB, stride=2), :] = summed[:HB]
    grad_ref[pl.ds(1, HB, stride=2), :] = summed[HB:]

    g_step(HALF_Y - 1)
    projected += term(HALF_Y - 1)
    projected += term(HALF_Y + 1)
    projected += term(HALF_Y)
    proj_ref[...] = projected.astype(jnp.bfloat16)

    for copy in gz:
        copy.wait_send()
    for k in range(NY):
        sib_copy(k).wait_send()
        gs_copy(k).wait_send()
    for s in range(HALF_Y):
        r_copy(s).wait_send()
        l_copy(s).wait_send()
        g_copy(0, s).wait_send()
        g_copy(1, s).wait_send()
    for j in range(NZ - 1):
        z_copy(j).wait_send()
    for j in range(NZH - 1):
        h_copy(j).wait_send()
    for j in range(NX - 1):
        x_copy(j).wait_send()


def on_device(tokens, cotangent, weight_codes, weight_scales, rounding_table, stream_offsets):
    dma = pltpu.SemaphoreType.DMA
    bf16, f32 = jnp.bfloat16, jnp.float32
    column = (NZ, ROWS, HD)
    scratch = [
        pltpu.VMEM((TOK, NY * CHUNK), bf16),
        pltpu.VMEM((TOK, HD), bf16),
        pltpu.VMEM((ROWS, HD), bf16),
        pltpu.VMEM((NY * CHUNK, HD), jnp.int32),
        pltpu.VMEM((CHUNK, HD), f32),
        pltpu.VMEM((NY,) + column, f32),
        pltpu.VMEM((NY,) + column, bf16),
        pltpu.VMEM((NY,) + column, bf16),
        pltpu.VMEM((HALF_Y,) + column, bf16),
        pltpu.VMEM((HALF_Y,) + column, bf16),
        pltpu.VMEM((HALF_Y,) + column, bf16),
        pltpu.VMEM((HALF_Y,) + column, bf16),
        pltpu.VMEM(column, bf16),
        pltpu.VMEM((NZ - 1, ROWS, HD), bf16),
        pltpu.VMEM((NZH, ROWS, HD), bf16),
        pltpu.VMEM((NX, ROWS, HD), bf16),
        pltpu.VMEM((NY, NZ, 2, ROWS, HD), bf16),
        dma((NY,)), dma((NY,)), dma((2,)), dma((NY,)), dma((NY,)),
        dma((HALF_Y,)), dma((HALF_Y,)), dma((HALF_Y,)), dma((HALF_Y,)),
        dma((NZ - 1,)), dma((NZ - 1,)), dma((NZH - 1,)), dma((NZH - 1,)),
        dma((NX - 1,)), dma((NX - 1,)), dma((NZ - 1,)), dma((NZ - 1,)),
        dma((HALF_Y,)), dma((HALF_Y,)), dma((HALF_Y,)), dma((HALF_Y,)),
        dma((NY,)), dma((NY,)),
    ]
    anywhere = pl.BlockSpec(memory_space=pl.ANY)
    vmem = pl.BlockSpec(memory_space=pltpu.VMEM)
    return pl.pallas_call(
        kernel,
        out_shape=(
            jax.ShapeDtypeStruct((TOK, HD), bf16),
            jax.ShapeDtypeStruct((ROWS, HD), f32),
        ),
        in_specs=[anywhere, anywhere, anywhere, vmem, anywhere,
                  pl.BlockSpec(memory_space=pltpu.SMEM)],
        out_specs=(vmem, vmem),
        scratch_shapes=scratch,
        compiler_params=pltpu.CompilerParams(
            collective_id=0, has_side_effects=True, vmem_limit_bytes=48 * 2**20
        ),
        cost_estimate=pl.CostEstimate(
            flops=4 * TOK * NY * CHUNK * HD, bytes_accessed=9 * 2**20, transcendentals=0
        ),
    )(tokens, cotangent, weight_codes, weight_scales.reshape(1, HB), rounding_table, stream_offsets)


def solution(mesh):
    assert dict(mesh.shape) == {"node": NX * NZH, "local": NY * NZ * 2}
    in_specs = (
        P(("node", "local"), None),
        P(("node", "local"), None),
        P("local", None),
        P("local"),
        P(),
        P(("node", "local")),
    )
    out_specs = (P(("node", "local"), None), P("local", None))
    return jax.shard_map(
        on_device, mesh=mesh, in_specs=in_specs, out_specs=out_specs, check_vma=False
    )
```

time: 417 us -> 63.6 us (0.15)
  the two profiles are of different devices: /device:TPU:8 before, /device:TPU:1 now
where the time goes in v1:
time: 63.6 us; the launch traced here: 63.3 us
  Pallas kernels  56.3 us (89%)
  local copies, waits for them, and re-layouts  5.69 us (9%)
  between operations  1.3 us (2%)
    pallas_call x1, Pallas kernels, on_device(): pl.pallas_call(kernel, out_shape=(jax.ShapeDtypeStruct((TOK, HD), bf16),...  56.3 us
    unnamed x10, local copies, waits for them, and re-layouts  5.69 us

profile of v1, /device:TPU:1, one launch (start us, length us, event | category | flops | bytes accessed | tf_op | source)
XLA Modules:
  0.0 63.3 jit_solution(8926648219378385928)
XLA Ops:
  1.3 0.0 copy-start
  1.3 2.2 %copy-done = bf16[256,8192]{1,0:T(8,128)(2,1)S(1)} copy-done((bf16[256,8192]{1,0:T(8,128)(2,1)S(1)}, bf16[256,8192]{1,0:T(8,128)(2,1)}, u32[]{:S(2)}) %copy-start) | copy-done | bytes 4194328
  3.5 0.0 copy-start.1
  3.5 0.8 %copy-done.1 = bf16[256,128]{1,0:T(8,128)(2,1)S(1)} copy-done((bf16[256,128]{1,0:T(8,128)(2,1)S(1)}, bf16[256,128]{1,0:T(8,128)(2,1)}, u32[]{:S(2)}) %copy-start.1) | copy-done | bytes 65560
  4.3 0.0 copy-start.2
  4.3 0.8 %copy-done.2 = bf16[128,128]{1,0:T(8,128)(2,1)S(1)} copy-done((bf16[128,128]{1,0:T(8,128)(2,1)S(1)}, bf16[128,128]{1,0:T(8,128)(2,1)}, u32[]{:S(2)}) %copy-start.2) | copy-done | bytes 32792
  5.1 0.0 copy-start.3
  5.1 0.7 %copy-done.3 = bf16[64]{0:T(256)(128)(2,1)S(1)} copy-done((bf16[64]{0:T(256)(128)(2,1)S(1)}, bf16[64]{0:T(256)(128)(2,1)}, u32[]{:S(2)}) %copy-start.3) | copy-done | bytes 152
  5.7 56.3 %shard_map.77 = (bf16[256,128]{1,0:T(8,128)(2,1)S(1)}, f32[128,128]{1,0:T(8,128)S(1)}) custom-call(bf16[256,8192]{1,0:T(8,128)(2,1)S(1)} %copy-done, bf16[256,128]{1,0:T(8,128)(2,1)S(1)} %copy-done.1, bf16[128,128]{1,0:T(8,128)(2,1)S(1)} %copy-done.2, bf16[1,64]{1,0:T(2,128)(2,1)S(1)} %bitcast.1, s32[8192,128]{1,0:T(8,128)} %table_hbm.1, s32[1]{0:T(128)S(6)} %copy.10.off_ref), custom_call_target="tpu_custom_call" | custom-call | flops 1073741824 | bytes 9437184 | tf_op jit(solution)/shard_map/pallas_call | solution.py:362
  62.0 0.6 copy.11
  62.6 0.6 copy.12
Async XLA Ops:
  1.3 2.2 %copy-start = (bf16[256,8192]{1,0:T(8,128)(2,1)S(1)}, bf16[256,8192]{1,0:T(8,128)(2,1)}, u32[]{:S(2)}) copy-start(bf16[256,8192]{1,0:T(8,128)(2,1)} %tok_hbm.1) | copy-start | bytes 12582916
  3.5 0.8 %copy-start.1 = (bf16[256,128]{1,0:T(8,128)(2,1)S(1)}, bf16[256,128]{1,0:T(8,128)(2,1)}, u32[]{:S(2)}) copy-start(bf16[256,128]{1,0:T(8,128)(2,1)} %cot_hbm.1) | copy-start | bytes 196612
  4.3 0.8 %copy-start.2 = (bf16[128,128]{1,0:T(8,128)(2,1)S(1)}, bf16[128,128]{1,0:T(8,128)(2,1)}, u32[]{:S(2)}) copy-start(bf16[128,128]{1,0:T(8,128)(2,1)} %wc_hbm.1) | copy-start | bytes 98308
  5.1 0.7 %copy-start.3 = (bf16[64]{0:T(256)(128)(2,1)S(1)}, bf16[64]{0:T(256)(128)(2,1)}, u32[]{:S(2)}) copy-start(bf16[64]{0:T(256)(128)(2,1)} %param.9) | copy-start | bytes 388

commit v2 on v1

v2 whole, which is shorter than its diff:
```python
import jax
import jax.numpy as jnp
from jax import lax
from jax.experimental import pallas as pl
from jax.experimental.pallas import tpu as pltpu
from jax.sharding import PartitionSpec as P

MESH = pl.DeviceIdType.MESH
EPS = 1e-06
HEADROOM = 1.0078125
GRAD_TOP = 7.0
NODE_TOP = 127.0

NX, NZH, NY, NZ = 4, 3, 8, 4
HALF_Y = NY // 2
ROWS = 128
HD = 128
HB = ROWS // 2
CHUNK = NZ * 2 * ROWS
TOK = 256
HALF_Z = NZ // 2
VMEM_LIMIT = 60 * 2**20
AHEAD = 3


def block_scale(even, odd, top):
    largest = jnp.max(jnp.maximum(jnp.abs(even), jnp.abs(odd)), axis=1, keepdims=True)
    return ((largest + EPS) * HEADROOM / top).astype(jnp.bfloat16).astype(jnp.float32)


def kernel(
    tok_hbm, cot_hbm, wc_hbm, ws_hbm, table_hbm, off_ref,
    proj_ref, grad_ref,
    tok, cot, wc, ws, table, part, own, sib_out, sib_in, r_out, r_in, l_out, l_in,
    z_out, z_in, h_buf, x_buf, w_buf,
    tok_sem, table_sem, small_sem, sib_ss, sib_rs, r_ss, r_rs, l_ss, l_rs,
    z_ss, z_rs, h_ss, h_rs, x_ss, x_rs, gz_ss, gz_rs, gr_ss, gr_rs, gl_ss, gl_rs,
    gx_ss, gx_rs, gs_ss, gs_rs, later_h,
):
    node = lax.axis_index("node")
    local = lax.axis_index("local")
    x, zh = node // NZH, node % NZH
    y, z, core = local // (NZ * 2), (local // 2) % NZ, local % 2
    other = 1 - core

    def at(y_, z_, c_):
        return (node, (y_ * NZ + z_) * 2 + c_)

    def up(step):
        return at((y + step) % NY, z, core)

    def down(step):
        return at((y + NY - step) % NY, z, core)

    sibling = at(y, z, other)
    x_peers = [(((x + j) % NX) * NZH + zh, local) for j in range(1, NX)]
    z_peers = [at(y, (z + j) % NZ, core) for j in range(1, NZ)]
    near = [sibling, up(1), down(1)] + z_peers + x_peers

    def h_peer(zh_):
        return (x * NZH + zh_, local)

    def signal(sem, peer):
        pl.semaphore_signal(sem, inc=1, device_id=peer, device_id_type=MESH)

    barrier = pltpu.get_barrier_semaphore()
    for peer in near:
        signal(barrier, peer)
    for zh_ in range(1, NZH):
        @pl.when(zh < zh_)
        def _():
            signal(barrier, h_peer(zh_))

    order = [(y + HALF_Y) % NY]
    for far in range(HALF_Y - 1, 0, -1):
        order += [(y + far) % NY, (y + NY - far) % NY]
    order += [y]

    def tok_copy(k):
        cols = pl.ds(pl.multiple_of(order[k] * CHUNK, CHUNK), CHUNK)
        return pltpu.make_async_copy(tok_hbm.at[:, cols], tok.at[:, cols], tok_sem.at[k])

    def table_copy(k):
        rows = pl.ds(pl.multiple_of(order[k] * CHUNK, CHUNK), CHUNK)
        return pltpu.make_async_copy(table_hbm.at[rows], table.at[rows], table_sem.at[k])

    def fetch(k):
        tok_copy(k).start()
        table_copy(k).start()

    cot_copy = pltpu.make_async_copy(cot_hbm, cot, small_sem.at[0])
    wc_copy = pltpu.make_async_copy(wc_hbm, wc, small_sem.at[1])
    ws_copy = pltpu.make_async_copy(ws_hbm, ws, small_sem.at[2])
    cot_copy.start()
    fetch(0)
    wc_copy.start()
    ws_copy.start()
    for k in range(1, AHEAD):
        fetch(k)

    def remote(src, dst, ss, rs, dev):
        return pltpu.make_async_remote_copy(
            src_ref=src, dst_ref=dst, send_sem=ss, recv_sem=rs, device_id=dev, device_id_type=MESH
        )

    offset = off_ref[0]

    def quantized(block, core_of, base):
        start = pl.multiple_of((block * 2 + core_of) * ROWS, ROWS)
        even = part[pl.ds(start, HB, stride=2), :]
        odd = part[pl.ds(start + 1, HB, stride=2), :]
        scale = block_scale(even, odd, GRAD_TOP)
        inverse = 1.0 / scale
        out = []
        for parity, value in ((0, even), (1, odd)):
            draws = table[pl.ds(base + start + parity, HB, stride=2), :]
            draws = ((draws + offset) & 1023).astype(jnp.float32)
            shift = draws * (1.0 / 1024.0) + (0.5 / 1024.0 - 0.5)
            codes = (value * inverse + shift).astype(jnp.bfloat16)
            out.append(codes.astype(jnp.float32) * scale)
        return out

    def sib_copy(k):
        return remote(sib_out.at[k], sib_in.at[k], sib_ss.at[k], sib_rs.at[k], sibling)

    def compute(k, ready=None):
        tok_copy(k).wait()
        table_copy(k).wait()
        if k + AHEAD < NY:
            fetch(k + AHEAD)
        base = pl.multiple_of(order[k] * CHUNK, CHUNK)
        part[...] = lax.dot_general(
            tok[:, pl.ds(base, CHUNK)], cot[...], (((0,), (0,)), ((), ())),
            preferred_element_type=jnp.float32,
        )
        for block in range(NZ):
            even, odd = quantized(block, other, base)
            sib_out[k, block, :HB] = even.astype(jnp.bfloat16)
            sib_out[k, block, HB:] = odd.astype(jnp.bfloat16)
        if ready is not None:
            ready()
        if k > 0:
            sib_copy(k).start()
        for block in range(NZ):
            even, odd = quantized(block, core, base)
            own[k, block, :HB] = even
            own[k, block, HB:] = odd

    def ring_copy(way, s, q):
        out, came, ss, rs, dev = (
            (r_out, r_in, r_ss, r_rs, up(1)) if way == 0 else (l_out, l_in, l_ss, l_rs, down(1))
        )
        return remote(out.at[s, q], came.at[s, q], ss.at[s, q], rs.at[s, q], dev)

    ways = (range(HALF_Z), range(HALF_Z, NZ))

    def pass_on(way, s, part_of):
        k = 0 if s == 0 else 2 * s - 1 + way
        out, came = (r_out, r_in) if way == 0 else (l_out, l_in)
        for q in ways[part_of]:
            total = own[k, q] + sib_in[k, q].astype(jnp.float32)
            if s > 1 or (s == 1 and part_of == way):
                ring_copy(way, s - 1, q).wait_recv()
                total += came[s - 1, q].astype(jnp.float32)
            out[s, q] = total.astype(jnp.bfloat16)
            ring_copy(way, s, q).start()

    def gz_copy(j):
        piece = w_buf.at[y, z, core, x]
        return remote(piece, piece, gz_ss.at[j], gz_rs.at[j], z_peers[j])

    def gz_came(j):
        piece = w_buf.at[y, (z + NZ - 1 - j) % NZ, core, x]
        return remote(piece, piece, gz_ss.at[j], gz_rs.at[j], sibling)

    def gy_copy(way, s):
        if way == 0:
            piece = w_buf.at[(y + NY - s) % NY, :, core, x]
            return remote(piece, piece, gr_ss.at[s], gr_rs.at[s], up(1))
        piece = w_buf.at[(y + s) % NY, :, core, x]
        return remote(piece, piece, gl_ss.at[s], gl_rs.at[s], down(1))

    def gy_came(way, s):
        if way == 0:
            piece = w_buf.at[(y + NY - s - 1) % NY, :, core, x]
            return remote(piece, piece, gr_ss.at[s], gr_rs.at[s], sibling)
        piece = w_buf.at[(y + s + 1) % NY, :, core, x]
        return remote(piece, piece, gl_ss.at[s], gl_rs.at[s], sibling)

    def gx_copy(r, j):
        piece = w_buf.at[(y + r) % NY, :, core, x]
        return remote(piece, piece, gx_ss.at[r, j], gx_rs.at[r, j], x_peers[j])

    def gx_came(r, j):
        piece = w_buf.at[(y + r) % NY, :, core, (x + NX - 1 - j) % NX]
        return remote(piece, piece, gx_ss.at[r, j], gx_rs.at[r, j], sibling)

    def gs_copy(r):
        piece = w_buf.at[(y + r) % NY, :, core]
        return remote(piece, piece, gs_ss.at[r], gs_rs.at[r], sibling)

    def gs_came(r):
        piece = w_buf.at[(y + r) % NY, :, other]
        return remote(piece, piece, gs_ss.at[r], gs_rs.at[r], sibling)

    def gx_send(r):
        for j in range(NX - 1):
            gx_copy(r, j).start()

    def g_step(s):
        if s >= 0:
            gy_came(0, s).wait_recv()
            if s < HALF_Y - 1:
                gy_came(1, s).wait_recv()
        else:
            for j in range(NZ - 1):
                gz_came(j).wait_recv()
        if s + 1 < HALF_Y:
            gy_copy(0, s + 1).start()
        if s + 1 < HALF_Y - 1:
            gy_copy(1, s + 1).start()
        gx_send((NY - s - 1) % NY)
        if 0 <= s < HALF_Y - 1:
            gx_send(s + 1)

    def to_sibling(rows):
        for r in rows:
            for j in range(NX - 1):
                gx_came(r, j).wait_recv()
            gs_copy(r).start()

    near_rows, far_rows = (0, NY - 1, 1, NY - 2, 2), (NY - 3, 3, HALF_Y)

    wc_copy.wait()
    ws_copy.wait()
    row = lax.broadcasted_iota(jnp.int32, (ROWS, HB), 0)
    col = lax.broadcasted_iota(jnp.int32, (ROWS, HB), 1)
    spread = jnp.broadcast_to(ws[...].astype(jnp.float32), (ROWS, HB))
    w_scale = jnp.sum(jnp.where(row // 2 == col, spread, 0.0), axis=1, keepdims=True)
    wc[...] = (wc[...].astype(jnp.float32) * w_scale).astype(jnp.bfloat16)
    quarter = ROWS // NX
    w_buf[y, z, core, x] = wc[pl.ds(pl.multiple_of(x * quarter, quarter), quarter)]

    def enter():
        pl.semaphore_wait(barrier, len(near) + zh)
        for j in range(NZ - 1):
            gz_copy(j).start()
        for zh_ in range(NZH - 1):
            @pl.when(zh_ < zh)
            def _():
                signal(later_h, h_peer(zh_))

    def first_sends():
        enter()
        sib_copy(0).start()

    cot_copy.wait()
    compute(0)
    compute(1, first_sends)
    sib_copy(0).wait_recv()
    pass_on(0, 0, 0)
    pass_on(1, 0, 1)
    compute(2)
    sib_copy(1).wait_recv()
    pass_on(0, 1, 1)
    compute(3)
    sib_copy(2).wait_recv()
    pass_on(1, 1, 0)
    g_step(-1)
    compute(4)
    sib_copy(3).wait_recv()
    pass_on(0, 1, 0)
    pass_on(1, 1, 1)
    g_step(0)
    compute(5)
    sib_copy(4).wait_recv()
    pass_on(0, 2, 1)
    pass_on(1, 2, 0)
    compute(6)
    sib_copy(5).wait_recv()
    pass_on(0, 2, 0)
    pass_on(1, 2, 1)
    g_step(1)
    compute(7)
    sib_copy(6).wait_recv()
    pass_on(0, 3, 1)
    pass_on(1, 3, 0)
    pass_on(0, 3, 0)
    pass_on(1, 3, 1)
    sib_copy(7).wait_recv()

    g_step(2)

    last = HALF_Y - 1

    def z_copy(z_):
        return remote(z_out.at[z_], z_in.at[z], z_ss.at[z_], z_rs.at[z], at(y, z_, core))

    def z_came(z_):
        return remote(z_out.at[z_], z_in.at[z_], z_ss.at[z_], z_rs.at[z_], sibling)

    for q in range(NZ):
        ring_copy(0, last, q).wait_recv()
        ring_copy(1, last, q).wait_recv()
        total = own[NY - 1, q] + sib_in[NY - 1, q].astype(jnp.float32)
        total += r_in[last, q].astype(jnp.float32) + l_in[last, q].astype(jnp.float32)
        own[NY - 1, q] = total
        z_out[q] = total.astype(jnp.bfloat16)

        @pl.when(q != z)
        def _():
            z_copy(q).start()

    node_total = own[NY - 1, z]
    for j in range(1, NZ):
        z_ = (z + j) % NZ
        z_came(z_).wait_recv()
        node_total += z_in[z_].astype(jnp.float32)
    even, odd = node_total[:HB], node_total[HB:]
    scale = block_scale(even, odd, NODE_TOP)
    inverse = 1.0 / scale
    for at_row, value in ((0, even), (HB, odd)):
        codes = (value * inverse).astype(jnp.bfloat16)
        h_buf[zh, at_row:at_row + HB] = (codes.astype(jnp.float32) * scale).astype(jnp.bfloat16)

    def h_copy(j):
        return remote(
            h_buf.at[zh], h_buf.at[zh], h_ss.at[j], h_rs.at[j], h_peer((zh + j + 1) % NZH)
        )

    def h_came(j):
        dst = h_buf.at[(zh + NZH - 1 - j) % NZH]
        return remote(dst, dst, h_ss.at[j], h_rs.at[j], sibling)

    @pl.when(zh < NZH - 1)
    def _():
        pl.semaphore_wait(later_h, NZH - 1 - zh)

    for j in range(NZH - 1):
        h_copy(j).start()

    g_step(3)
    to_sibling(near_rows)
    to_sibling(far_rows)

    def term(r):
        gs_came(r).wait_recv()
        b = (y + r) % NY
        dense = w_buf[b].reshape(CHUNK, HD)
        cols = pl.ds(pl.multiple_of(b * CHUNK, CHUNK), CHUNK)
        return jnp.dot(tok[:, cols], dense, preferred_element_type=jnp.float32)

    projected = term(0) + term(NY - 1) + term(1)

    for j in range(NZH - 1):
        h_came(j).wait_recv()
    summed = h_buf[0].astype(jnp.float32)
    for i in range(1, NZH):
        summed += h_buf[i].astype(jnp.float32)
    x_buf[x] = summed.astype(jnp.bfloat16)

    def x_copy(j):
        return remote(x_buf.at[x], x_buf.at[x], x_ss.at[j], x_rs.at[j], x_peers[j])

    def x_came(j):
        dst = x_buf.at[(x + NX - 1 - j) % NX]
        return remote(dst, dst, x_ss.at[j], x_rs.at[j], sibling)

    for j in range(NX - 1):
        x_copy(j).start()

    for r in (NY - 2, 2) + far_rows:
        projected += term(r)
    proj_ref[...] = projected.astype(jnp.bfloat16)

    for k in range(NY):
        sib_copy(k).wait_send()
        gs_copy(k).wait_send()
        for j in range(NX - 1):
            gx_copy(k, j).wait_send()
    for s in range(HALF_Y):
        for q in range(NZ):
            for way in range(2):
                if s > 0 or q in ways[way]:
                    ring_copy(way, s, q).wait_send()
    for s in range(HALF_Y):
        gy_copy(0, s).wait_send()
    for s in range(HALF_Y - 1):
        gy_copy(1, s).wait_send()
    for j in range(NZ - 1):
        gz_copy(j).wait_send()
        z_copy((z + j + 1) % NZ).wait_send()
    for j in range(NZH - 1):
        h_copy(j).wait_send()

    for j in range(NX - 1):
        x_came(j).wait_recv()
    summed = x_buf[0].astype(jnp.float32)
    for i in range(1, NX):
        summed += x_buf[i].astype(jnp.float32)
    grad_ref[pl.ds(0, HB, stride=2), :] = summed[:HB]
    grad_ref[pl.ds(1, HB, stride=2), :] = summed[HB:]
    for j in range(NX - 1):
        x_copy(j).wait_send()


def settle(p_ref, g_ref, proj_ref, grad_ref):
    proj_ref[...] = p_ref[...]
    grad_ref[...] = g_ref[...]


def on_device(tokens, cotangent, weight_codes, weight_scales, rounding_table, stream_offsets):
    dma = pltpu.SemaphoreType.DMA
    bf16, f32 = jnp.bfloat16, jnp.float32
    column = (NZ, ROWS, HD)
    scratch = [
        pltpu.VMEM((TOK, NY * CHUNK), bf16),
        pltpu.VMEM((TOK, HD), bf16),
        pltpu.VMEM((ROWS, HD), bf16),
        pltpu.VMEM((1, HB), bf16),
        pltpu.VMEM((NY * CHUNK, HD), jnp.int32),
        pltpu.VMEM((CHUNK, HD), f32),
        pltpu.VMEM((NY,) + column, f32),
        pltpu.VMEM((NY,) + column, bf16),
        pltpu.VMEM((NY,) + column, bf16),
        pltpu.VMEM((HALF_Y,) + column, bf16),
        pltpu.VMEM((HALF_Y,) + column, bf16),
        pltpu.VMEM((HALF_Y,) + column, bf16),
        pltpu.VMEM((HALF_Y,) + column, bf16),
        pltpu.VMEM(column, bf16),
        pltpu.VMEM(column, bf16),
        pltpu.VMEM((NZH, ROWS, HD), bf16),
        pltpu.VMEM((NX, ROWS, HD), bf16),
        pltpu.VMEM((NY, NZ, 2, NX, ROWS // NX, HD), bf16),
        dma((NY,)), dma((NY,)), dma((3,)), dma((NY,)), dma((NY,)),
        dma((HALF_Y, NZ)), dma((HALF_Y, NZ)), dma((HALF_Y, NZ)), dma((HALF_Y, NZ)),
        dma((NZ,)), dma((NZ,)), dma((NZH - 1,)), dma((NZH - 1,)), dma((NX - 1,)), dma((NX - 1,)),
        dma((NZ - 1,)), dma((NZ - 1,)),
        dma((HALF_Y,)), dma((HALF_Y,)), dma((HALF_Y,)), dma((HALF_Y,)),
        dma((NY, NX - 1)), dma((NY, NX - 1)),
        dma((NY,)), dma((NY,)),
        pltpu.SemaphoreType.REGULAR,
    ]
    hbm = pl.BlockSpec(memory_space=pltpu.MemorySpace.HBM)
    vmem = pl.BlockSpec(memory_space=pltpu.VMEM)
    out_shape = (
        jax.ShapeDtypeStruct((TOK, HD), bf16),
        jax.ShapeDtypeStruct((ROWS, HD), f32),
    )
    results = pl.pallas_call(
        kernel,
        out_shape=out_shape,
        in_specs=[hbm, hbm, hbm, hbm, hbm, pl.BlockSpec(memory_space=pltpu.SMEM)],
        out_specs=(vmem, vmem),
        scratch_shapes=scratch,
        compiler_params=pltpu.CompilerParams(
            collective_id=0, has_side_effects=True, vmem_limit_bytes=VMEM_LIMIT
        ),
        cost_estimate=pl.CostEstimate(
            flops=4 * TOK * NY * CHUNK * HD, bytes_accessed=9 * 2**20, transcendentals=0
        ),
    )(tokens, cotangent, weight_codes, weight_scales.reshape(1, HB), rounding_table, stream_offsets)
    return pl.pallas_call(
        settle,
        out_shape=out_shape,
        in_specs=[vmem, vmem],
        out_specs=(vmem, vmem),
        compiler_params=pltpu.CompilerParams(vmem_limit_bytes=VMEM_LIMIT),
    )(*results)


def solution(mesh):
    assert dict(mesh.shape) == {"node": NX * NZH, "local": NY * NZ * 2}
    in_specs = (
        P(("node", "local"), None),
        P(("node", "local"), None),
        P("local", None),
        P("local"),
        P(),
        P(("node", "local")),
    )
    out_specs = (P(("node", "local"), None), P("local", None))
    return jax.shard_map(
        on_device, mesh=mesh, in_specs=in_specs, out_specs=out_specs, check_vma=False
    )
```

time: 63.6 us -> 52.7 us (0.83)
  the two profiles are of different devices: /device:TPU:1 before, /device:TPU:24 now
where the time goes in v2:
time: 52.7 us; the launch traced here: 52.5 us
  Pallas kernels  51.2 us (97%)
  between operations  1.29 us (2%)
    pallas_call x1, Pallas kernels, on_device(): pl.pallas_call(kernel, out_shape=out_shape, in_specs=[hbm, hbm, hbm, hbm,...  49.7 us
    pallas_call x1, Pallas kernels, on_device(): pl.pallas_call(settle, out_shape=out_shape, in_specs=[vmem, vmem], out_sp...  1.53 us

profile of v2, /device:TPU:24, one launch (start us, length us, event | category | flops | bytes accessed | tf_op | source)
XLA Modules:
  0.0 52.5 jit_solution(13349160367841559914)
XLA Ops:
  1.3 49.7 %shard_map.77 = (bf16[256,128]{1,0:T(8,128)(2,1)}, f32[128,128]{1,0:T(8,128)}) custom-call(bf16[256,8192]{1,0:T(8,128)(2,1)} %tok_hbm.1, bf16[256,128]{1,0:T(8,128)(2,1)} %cot_hbm.1, bf16[128,128]{1,0:T(8,128)(2,1)} %wc_hbm.1, bf16[1,64]{1,0:T(2,128)(2,1)} %bitcast.1, s32[8192,128]{1,0:T(8,128)} %table_hbm.1, s32[1]{0:T(128)S(6)} %copy.8.off_ref), custom_call_target="tpu_custom_call" | custom-call | flops 1073741824 | bytes 9437184 | tf_op jit(solution)/shard_map/pallas_call | solution.py:450
  51.0 1.5 %shard_map.78 = (bf16[256,128]{1,0:T(8,128)(2,1)}, f32[128,128]{1,0:T(8,128)}) custom-call(bf16[256,128]{1,0:T(8,128)(2,1)} %get-tuple-element.4.p_ref, f32[128,128]{1,0:T(8,128)} %get-tuple-element.5.g_ref), custom_call_target="tpu_custom_call" | custom-call | tf_op jit(solution)/shard_map/pallas_call | solution.py:463

commit v3 on v2

--- a/solution.py
+++ b/solution.py
@@ -165,27 +165,27 @@
             out[s, q] = total.astype(jnp.bfloat16)
             ring_copy(way, s, q).start()
 
-    def gz_copy(j):
-        piece = w_buf.at[y, z, core, x]
-        return remote(piece, piece, gz_ss.at[j], gz_rs.at[j], z_peers[j])
-
-    def gz_came(j):
-        piece = w_buf.at[y, (z + NZ - 1 - j) % NZ, core, x]
-        return remote(piece, piece, gz_ss.at[j], gz_rs.at[j], sibling)
-
     def gy_copy(way, s):
         if way == 0:
-            piece = w_buf.at[(y + NY - s) % NY, :, core, x]
+            piece = w_buf.at[(y + NY - s) % NY, z, core, x]
             return remote(piece, piece, gr_ss.at[s], gr_rs.at[s], up(1))
-        piece = w_buf.at[(y + s) % NY, :, core, x]
+        piece = w_buf.at[(y + s) % NY, z, core, x]
         return remote(piece, piece, gl_ss.at[s], gl_rs.at[s], down(1))
 
     def gy_came(way, s):
         if way == 0:
-            piece = w_buf.at[(y + NY - s - 1) % NY, :, core, x]
+            piece = w_buf.at[(y + NY - s - 1) % NY, z, core, x]
             return remote(piece, piece, gr_ss.at[s], gr_rs.at[s], sibling)
-        piece = w_buf.at[(y + s + 1) % NY, :, core, x]
+        piece = w_buf.at[(y + s + 1) % NY, z, core, x]
         return remote(piece, piece, gl_ss.at[s], gl_rs.at[s], sibling)
+
+    def gz_copy(r, j):
+        piece = w_buf.at[(y + r) % NY, z, core, x]
+        return remote(piece, piece, gz_ss.at[r, j], gz_rs.at[r, j], z_peers[j])
+
+    def gz_came(r, j):
+        piece = w_buf.at[(y + r) % NY, (z + NZ - 1 - j) % NZ, core, x]
+        return remote(piece, piece, gz_ss.at[r, j], gz_rs.at[r, j], sibling)
 
     def gx_copy(r, j):
         piece = w_buf.at[(y + r) % NY, :, core, x]
@@ -203,33 +203,41 @@
         piece = w_buf.at[(y + r) % NY, :, other]
         return remote(piece, piece, gs_ss.at[r], gs_rs.at[r], sibling)
 
-    def gx_send(r):
-        for j in range(NX - 1):
-            gx_copy(r, j).start()
+    def along_y(s):
+        if s < HALF_Y:
+            gy_copy(0, s).start()
+        if s < HALF_Y - 1:
+            gy_copy(1, s).start()
+
+    def along_z(rows):
+        for r in rows:
+            for j in range(NZ - 1):
+                gz_copy(r, j).start()
+
+    def along_x(rows):
+        for r in rows:
+            for j in range(NZ - 1):
+                gz_came(r, j).wait_recv()
+            for j in range(NX - 1):
+                gx_copy(r, j).start()
+
+    near_rows, far_rows = (0, NY - 1, 1, NY - 2, 2), (NY - 3, 3, HALF_Y)
+
+    came_at = ((0,), (NY - 1, 1), (NY - 2, 2), (NY - 3, 3), (HALF_Y,))
 
     def g_step(s):
-        if s >= 0:
-            gy_came(0, s).wait_recv()
-            if s < HALF_Y - 1:
-                gy_came(1, s).wait_recv()
-        else:
-            for j in range(NZ - 1):
-                gz_came(j).wait_recv()
-        if s + 1 < HALF_Y:
-            gy_copy(0, s + 1).start()
-        if s + 1 < HALF_Y - 1:
-            gy_copy(1, s + 1).start()
-        gx_send((NY - s - 1) % NY)
-        if 0 <= s < HALF_Y - 1:
-            gx_send(s + 1)
+        gy_came(0, s).wait_recv()
+        if s < HALF_Y - 1:
+            gy_came(1, s).wait_recv()
+        along_y(s + 1)
+        along_z(came_at[s + 1])
+        along_x(came_at[s])
 
     def to_sibling(rows):
         for r in rows:
             for j in range(NX - 1):
                 gx_came(r, j).wait_recv()
             gs_copy(r).start()
-
-    near_rows, far_rows = (0, NY - 1, 1, NY - 2, 2), (NY - 3, 3, HALF_Y)
 
     wc_copy.wait()
     ws_copy.wait()
@@ -243,20 +251,17 @@
 
     def enter():
         pl.semaphore_wait(barrier, len(near) + zh)
-        for j in range(NZ - 1):
-            gz_copy(j).start()
+        sib_copy(0).start()
         for zh_ in range(NZH - 1):
             @pl.when(zh_ < zh)
             def _():
                 signal(later_h, h_peer(zh_))
-
-    def first_sends():
-        enter()
-        sib_copy(0).start()
+        along_y(0)
+        along_z((0,))
 
     cot_copy.wait()
     compute(0)
-    compute(1, first_sends)
+    compute(1, enter)
     sib_copy(0).wait_recv()
     pass_on(0, 0, 0)
     pass_on(1, 0, 1)
@@ -266,12 +271,11 @@
     compute(3)
     sib_copy(2).wait_recv()
     pass_on(1, 1, 0)
-    g_step(-1)
+    g_step(0)
     compute(4)
     sib_copy(3).wait_recv()
     pass_on(0, 1, 0)
     pass_on(1, 1, 1)
-    g_step(0)
     compute(5)
     sib_copy(4).wait_recv()
     pass_on(0, 2, 1)
@@ -311,6 +315,8 @@
         def _():
             z_copy(q).start()
 
+    g_step(3)
+
     node_total = own[NY - 1, z]
     for j in range(1, NZ):
         z_ = (z + j) % NZ
@@ -339,9 +345,8 @@
     for j in range(NZH - 1):
         h_copy(j).start()
 
-    g_step(3)
+    along_x(came_at[HALF_Y])
     to_sibling(near_rows)
-    to_sibling(far_rows)
 
     def term(r):
         gs_came(r).wait_recv()
@@ -350,34 +355,10 @@
         cols = pl.ds(pl.multiple_of(b * CHUNK, CHUNK), CHUNK)
         return jnp.dot(tok[:, cols], dense, preferred_element_type=jnp.float32)
 
-    projected = term(0) + term(NY - 1) + term(1)
-
-    for j in range(NZH - 1):
-        h_came(j).wait_recv()
-    summed = h_buf[0].astype(jnp.float32)
-    for i in range(1, NZH):
-        summed += h_buf[i].astype(jnp.float32)
-    x_buf[x] = summed.astype(jnp.bfloat16)
-
-    def x_copy(j):
-        return remote(x_buf.at[x], x_buf.at[x], x_ss.at[j], x_rs.at[j], x_peers[j])
-
-    def x_came(j):
-        dst = x_buf.at[(x + NX - 1 - j) % NX]
-        return remote(dst, dst, x_ss.at[j], x_rs.at[j], sibling)
-
-    for j in range(NX - 1):
-        x_copy(j).start()
-
-    for r in (NY - 2, 2) + far_rows:
-        projected += term(r)
-    proj_ref[...] = projected.astype(jnp.bfloat16)
-
     for k in range(NY):
         sib_copy(k).wait_send()
-        gs_copy(k).wait_send()
-        for j in range(NX - 1):
-            gx_copy(k, j).wait_send()
+        for j in range(NZ - 1):
+            gz_copy(k, j).wait_send()
     for s in range(HALF_Y):
         for q in range(NZ):
             for way in range(2):
@@ -388,8 +369,37 @@
     for s in range(HALF_Y - 1):
         gy_copy(1, s).wait_send()
     for j in range(NZ - 1):
-        gz_copy(j).wait_send()
         z_copy((z + j + 1) % NZ).wait_send()
+
+    for j in range(NZH - 1):
+        h_came(j).wait_recv()
+    summed = h_buf[0].astype(jnp.float32)
+    for i in range(1, NZH):
+        summed += h_buf[i].astype(jnp.float32)
+    x_buf[x] = summed.astype(jnp.bfloat16)
+
+    def x_copy(j):
+        return remote(x_buf.at[x], x_buf.at[x], x_ss.at[j], x_rs.at[j], x_peers[j])
+
+    def x_came(j):
+        dst = x_buf.at[(x + NX - 1 - j) % NX]
+        return remote(dst, dst, x_ss.at[j], x_rs.at[j], sibling)
+
+    for j in range(NX - 1):
+        x_copy(j).start()
+
+    to_sibling(far_rows)
+    projected = term(0)
+    for r in near_rows[1:]:
+        projected += term(r)
+    for k in range(NY):
+        for j in range(NX - 1):
+            gx_copy(k, j).wait_send()
+    for r in far_rows:
+        projected += term(r)
+    proj_ref[...] = projected.astype(jnp.bfloat16)
+    for k in range(NY):
+        gs_copy(k).wait_send()
     for j in range(NZH - 1):
         h_copy(j).wait_send()
 
@@ -435,7 +445,7 @@
         dma((NY,)), dma((NY,)), dma((3,)), dma((NY,)), dma((NY,)),
         dma((HALF_Y, NZ)), dma((HALF_Y, NZ)), dma((HALF_Y, NZ)), dma((HALF_Y, NZ)),
         dma((NZ,)), dma((NZ,)), dma((NZH - 1,)), dma((NZH - 1,)), dma((NX - 1,)), dma((NX - 1,)),
-        dma((NZ - 1,)), dma((NZ - 1,)),
+        dma((NY, NZ - 1)), dma((NY, NZ - 1)),
         dma((HALF_Y,)), dma((HALF_Y,)), dma((HALF_Y,)), dma((HALF_Y,)),
         dma((NY, NX - 1)), dma((NY, NX - 1)),
         dma((NY,)), dma((NY,)),

time: 52.7 us -> 51.2 us (0.972)
  the two profiles are of different devices: /device:TPU:24 before, /device:TPU:1 now
where the time goes in v3:
time: 51.2 us; the launch traced here: 50.9 us
  Pallas kernels  49.6 us (97%)
  between operations  1.29 us (3%)
    pallas_call x1, Pallas kernels, on_device(): pl.pallas_call(kernel, out_shape=out_shape, in_specs=[hbm, hbm, hbm, hbm,...  48.1 us
    pallas_call x1, Pallas kernels, on_device(): pl.pallas_call(settle, out_shape=out_shape, in_specs=[vmem, vmem], out_sp...  1.53 us

profile of v3, /device:TPU:1, one launch (start us, length us, event | category | flops | bytes accessed | tf_op | source)
XLA Modules:
  0.0 50.9 jit_solution(11927850131528305199)
XLA Ops:
  1.3 48.1 %shard_map.77 = (bf16[256,128]{1,0:T(8,128)(2,1)}, f32[128,128]{1,0:T(8,128)}) custom-call(bf16[256,8192]{1,0:T(8,128)(2,1)} %tok_hbm.1, bf16[256,128]{1,0:T(8,128)(2,1)} %cot_hbm.1, bf16[128,128]{1,0:T(8,128)(2,1)} %wc_hbm.1, bf16[1,64]{1,0:T(2,128)(2,1)} %bitcast.1, s32[8192,128]{1,0:T(8,128)} %table_hbm.1, s32[1]{0:T(128)S(6)} %copy.8.off_ref), custom_call_target="tpu_custom_call" | custom-call | flops 1073741824 | bytes 9437184 | tf_op jit(solution)/shard_map/pallas_call | solution.py:460
  49.3 1.5 %shard_map.78 = (bf16[256,128]{1,0:T(8,128)(2,1)}, f32[128,128]{1,0:T(8,128)}) custom-call(bf16[256,128]{1,0:T(8,128)(2,1)} %get-tuple-element.4.p_ref, f32[128,128]{1,0:T(8,128)} %get-tuple-element.5.g_ref), custom_call_target="tpu_custom_call" | custom-call | tf_op jit(solution)/shard_map/pallas_call | solution.py:473

commit v4 on v3

--- a/solution.py
+++ b/solution.py
@@ -325,25 +325,26 @@
     even, odd = node_total[:HB], node_total[HB:]
     scale = block_scale(even, odd, NODE_TOP)
     inverse = 1.0 / scale
-    for at_row, value in ((0, even), (HB, odd)):
+    parities = range(2)
+    for p, value in zip(parities, (even, odd)):
         codes = (value * inverse).astype(jnp.bfloat16)
-        h_buf[zh, at_row:at_row + HB] = (codes.astype(jnp.float32) * scale).astype(jnp.bfloat16)
-
-    def h_copy(j):
-        return remote(
-            h_buf.at[zh], h_buf.at[zh], h_ss.at[j], h_rs.at[j], h_peer((zh + j + 1) % NZH)
-        )
-
-    def h_came(j):
-        dst = h_buf.at[(zh + NZH - 1 - j) % NZH]
-        return remote(dst, dst, h_ss.at[j], h_rs.at[j], sibling)
+        h_buf[zh, p] = (codes.astype(jnp.float32) * scale).astype(jnp.bfloat16)
+
+    def h_copy(j, p):
+        mine = h_buf.at[zh, p]
+        return remote(mine, mine, h_ss.at[j, p], h_rs.at[j, p], h_peer((zh + j + 1) % NZH))
+
+    def h_came(j, p):
+        dst = h_buf.at[(zh + NZH - 1 - j) % NZH, p]
+        return remote(dst, dst, h_ss.at[j, p], h_rs.at[j, p], sibling)
 
     @pl.when(zh < NZH - 1)
     def _():
         pl.semaphore_wait(later_h, NZH - 1 - zh)
 
-    for j in range(NZH - 1):
-        h_copy(j).start()
+    for p in parities:
+        for j in range(NZH - 1):
+            h_copy(j, p).start()
 
     along_x(came_at[HALF_Y])
     to_sibling(near_rows)
@@ -371,22 +372,23 @@
     for j in range(NZ - 1):
         z_copy((z + j + 1) % NZ).wait_send()
 
-    for j in range(NZH - 1):
-        h_came(j).wait_recv()
-    summed = h_buf[0].astype(jnp.float32)
-    for i in range(1, NZH):
-        summed += h_buf[i].astype(jnp.float32)
-    x_buf[x] = summed.astype(jnp.bfloat16)
-
-    def x_copy(j):
-        return remote(x_buf.at[x], x_buf.at[x], x_ss.at[j], x_rs.at[j], x_peers[j])
-
-    def x_came(j):
-        dst = x_buf.at[(x + NX - 1 - j) % NX]
-        return remote(dst, dst, x_ss.at[j], x_rs.at[j], sibling)
-
-    for j in range(NX - 1):
-        x_copy(j).start()
+    def x_copy(j, p):
+        mine = x_buf.at[x, p]
+        return remote(mine, mine, x_ss.at[j, p], x_rs.at[j, p], x_peers[j])
+
+    def x_came(j, p):
+        dst = x_buf.at[(x + NX - 1 - j) % NX, p]
+        return remote(dst, dst, x_ss.at[j, p], x_rs.at[j, p], sibling)
+
+    for p in parities:
+        for j in range(NZH - 1):
+            h_came(j, p).wait_recv()
+        summed = h_buf[0, p].astype(jnp.float32)
+        for i in range(1, NZH):
+            summed += h_buf[i, p].astype(jnp.float32)
+        x_buf[x, p] = summed.astype(jnp.bfloat16)
+        for j in range(NX - 1):
+            x_copy(j, p).start()
 
     to_sibling(far_rows)
     projected = term(0)
@@ -400,18 +402,20 @@
     proj_ref[...] = projected.astype(jnp.bfloat16)
     for k in range(NY):
         gs_copy(k).wait_send()
-    for j in range(NZH - 1):
-        h_copy(j).wait_send()
-
-    for j in range(NX - 1):
-        x_came(j).wait_recv()
-    summed = x_buf[0].astype(jnp.float32)
-    for i in range(1, NX):
-        summed += x_buf[i].astype(jnp.float32)
-    grad_ref[pl.ds(0, HB, stride=2), :] = summed[:HB]
-    grad_ref[pl.ds(1, HB, stride=2), :] = summed[HB:]
-    for j in range(NX - 1):
-        x_copy(j).wait_send()
+    for p in parities:
+        for j in range(NZH - 1):
+            h_copy(j, p).wait_send()
+
+    for p in parities:
+        for j in range(NX - 1):
+            x_came(j, p).wait_recv()
+        summed = x_buf[0, p].astype(jnp.float32)
+        for i in range(1, NX):
+            summed += x_buf[i, p].astype(jnp.float32)
+        grad_ref[pl.ds(p, HB, stride=2), :] = summed
+    for p in parities:
+        for j in range(NX - 1):
+            x_copy(j, p).wait_send()
 
 
 def settle(p_ref, g_ref, proj_ref, grad_ref):
@@ -439,12 +443,12 @@
         pltpu.VMEM((HALF_Y,) + column, bf16),
         pltpu.VMEM(column, bf16),
         pltpu.VMEM(column, bf16),
-        pltpu.VMEM((NZH, ROWS, HD), bf16),
-        pltpu.VMEM((NX, ROWS, HD), bf16),
+        pltpu.VMEM((NZH, 2, HB, HD), bf16),
+        pltpu.VMEM((NX, 2, HB, HD), bf16),
         pltpu.VMEM((NY, NZ, 2, NX, ROWS // NX, HD), bf16),
         dma((NY,)), dma((NY,)), dma((3,)), dma((NY,)), dma((NY,)),
         dma((HALF_Y, NZ)), dma((HALF_Y, NZ)), dma((HALF_Y, NZ)), dma((HALF_Y, NZ)),
-        dma((NZ,)), dma((NZ,)), dma((NZH - 1,)), dma((NZH - 1,)), dma((NX - 1,)), dma((NX - 1,)),
+        dma((NZ,)), dma((NZ,)), dma((NZH - 1, 2)), dma((NZH - 1, 2)), dma((NX - 1, 2)), dma((NX - 1, 2)),
         dma((NY, NZ - 1)), dma((NY, NZ - 1)),
         dma((HALF_Y,)), dma((HALF_Y,)), dma((HALF_Y,)), dma((HALF_Y,)),
         dma((NY, NX - 1)), dma((NY, NX - 1)),

time: 51.2 us -> 51.2 us (level)
  no operation moved by 1% of the time
where the time goes in v4:
time: 51.2 us; the launch traced here: 51 us
  Pallas kernels  49.7 us (97%)
  between operations  1.29 us (3%)
    pallas_call x1, Pallas kernels, on_device(): pl.pallas_call(kernel, out_shape=out_shape, in_specs=[hbm, hbm, hbm, hbm,...  48.2 us
    pallas_call x1, Pallas kernels, on_device(): pl.pallas_call(settle, out_shape=out_shape, in_specs=[vmem, vmem], out_sp...  1.53 us

profile of v4, /device:TPU:1, one launch (start us, length us, event | category | flops | bytes accessed | tf_op | source)
XLA Modules:
  0.0 51.0 jit_solution(1810324288571974948)
XLA Ops:
  1.3 48.2 %shard_map.77 = (bf16[256,128]{1,0:T(8,128)(2,1)}, f32[128,128]{1,0:T(8,128)}) custom-call(bf16[256,8192]{1,0:T(8,128)(2,1)} %tok_hbm.1, bf16[256,128]{1,0:T(8,128)(2,1)} %cot_hbm.1, bf16[128,128]{1,0:T(8,128)(2,1)} %wc_hbm.1, bf16[1,64]{1,0:T(2,128)(2,1)} %bitcast.1, s32[8192,128]{1,0:T(8,128)} %table_hbm.1, s32[1]{0:T(128)S(6)} %copy.8.off_ref), custom_call_target="tpu_custom_call" | custom-call | flops 1073741824 | bytes 9437184 | tf_op jit(solution)/shard_map/pallas_call | solution.py:464
  49.4 1.5 %shard_map.78 = (bf16[256,128]{1,0:T(8,128)(2,1)}, f32[128,128]{1,0:T(8,128)}) custom-call(bf16[256,128]{1,0:T(8,128)(2,1)} %get-tuple-element.4.p_ref, f32[128,128]{1,0:T(8,128)} %get-tuple-element.5.g_ref), custom_call_target="tpu_custom_call" | custom-call | tf_op jit(solution)/shard_map/pallas_call | solution.py:477
